TPU v7x, 32 devices: a whole 2x2x4 slice. The times are simulated.
32 devices in a mesh: dp: 8 (over z, y), tensor: 4 (over x, core).
Axes of the slice: x: 2, y: 2, z: 4, core: 2. Of those that a mesh axis runs over, the one named last changes fastest.
Arguments:
- frames: bfloat16 [23552, 768], P('dp'), may hold values from -6 to 6
- segment_ids: int32 [32, 736], P('dp'), may hold values from 0 to 3, never falling along the last dimension, each value on 1 to 368 neighbouring positions
- valid_frames: int32 [32, 736], P('dp'), may hold values from 0 to 1, as said below
- inward_weight: bfloat16 [1, 3, 768, 768], P(None, None, None, 'tensor'), may hold values from -0.21875 to 0.21875
- inward_bias: bfloat16 [1, 2, 12, 64], P(None, None, 'tensor'), may hold values from -4 to 4
- output_weight: bfloat16 [1, 768, 768], P(None, 'tensor'), may hold values from -2 to 2
- upward_weight: bfloat16 [1, 768, 3072], P(None, None, 'tensor'), may hold values from -0.21875 to 0.21875
- upward_bias: bfloat16 [1, 24, 128], P(None, 'tensor'), may hold values from -4 to 4
- downward_weight: bfloat16 [1, 3072, 768], P(None, 'tensor'), may hold values from -0.109375 to 0.109375
- norm_gains: float32 [1, 2, 768], replicated, may hold values from 0.5 to 1.5
- offsets: float32 [1, 4, 768], replicated, may hold values from -4 to 4
- cotangent: float32 [23552, 768], P('dp'), may hold values from -6 to 6
Outputs:
- layer_output: bfloat16 [23552, 768], P('dp')
- grad_frames: float32 [23552, 768], P('dp')
- grad_inward_weight: float32 [1, 3, 768, 768], P(None, None, 'dp', 'tensor')
- grad_inward_bias: float32 [1, 2, 12, 64], P(None, None, 'tensor', 'dp')
- grad_output_weight: float32 [1, 768, 768], P(None, 'tensor', 'dp')
- grad_upward_weight: float32 [1, 768, 3072], P(None, 'dp', 'tensor')
- grad_upward_bias: float32 [1, 24, 128], P(None, 'tensor', 'dp')
- grad_downward_weight: float32 [1, 3072, 768], P(None, 'tensor', 'dp')
- grad_norm_gains: float32 [1, 2, 768], P(None, None, 'dp')
- grad_offsets: float32 [1, 4, 768], P(None, None, 'dp')
Inputs may be any that keep to these rules, and one draw needn't show every extreme that they name: `segment_ids`: within a row the clip numbers never fall; a clip holds at most 368 frames. `valid_frames`: in each row the frames that count come first and the padding last; at least 552 frames of a row count.
All inputs are finite; a program needn't handle non-finite values.
Results may differ from a plain program's by a relative error of at most 0.013.
The roundings to bfloat16 on the way count: a program that leaves them out, or rounds other values in their place, can miss the bound.
Values may be sent and summed in bfloat16 or wider, within the bound.
A program may use at most 192 MiB of HBM per device.

v0:
```python
import jax
import jax.numpy as jnp
from jax import lax
from jax.sharding import PartitionSpec as P

HEAD_SIZE = 64


epsilon = 1e-05
masked_score = -1000000000.0


def product(left_side, right_side):
    return jnp.dot(left_side, right_side, preferred_element_type=jnp.float32)


def contract_rows(left_side, right_side):
    return lax.dot_general(
        left_side, right_side, (((0,), (0,)), ((), ())), preferred_element_type=jnp.float32
    )


def contract_columns(left_side, right_side):
    return lax.dot_general(
        left_side, right_side, (((1,), (1,)), ((), ())), preferred_element_type=jnp.float32
    )


def layer_norm(values, gain, offset):
    centred = values - jnp.mean(values, axis=-1, keepdims=True)
    variance = jnp.mean(centred * centred, axis=-1, keepdims=True)
    return centred * lax.rsqrt(variance + epsilon) * gain + offset


def exact_gelu(values):
    return jax.nn.gelu(values, approximate=False)


def norm_backward(grad_rows, values, gain, offset):
    _, norm_pull = jax.vjp(layer_norm, values, gain, offset)
    return norm_pull(grad_rows)


def allowed_mask(segments, valid_mask):
    places = jnp.arange(segments.shape[0])
    same_clip = segments[:, None] == segments[None, :]
    return same_clip & ((valid_mask[None, :] > 0) | (places[:, None] == places[None, :]))


def split_heads(values):
    return values.reshape(values.shape[0], values.shape[1] // HEAD_SIZE, HEAD_SIZE)


def masked_scores(split_queries, split_keys, allowed):
    scores = (
        jnp.einsum("qhd,khd->hqk", split_queries, split_keys, preferred_element_type=jnp.float32)
        * 0.125
    )
    return jnp.where(allowed[None], scores, masked_score)


def attend_forward(packed):
    queries, key_rows, value_rows, allowed = packed
    scores = masked_scores(split_heads(queries), split_heads(key_rows), allowed)
    largest = jnp.max(scores, axis=-1, keepdims=True)
    weights = jnp.exp(scores - largest)
    denominator = jnp.sum(weights, axis=-1, keepdims=True)
    softmax_low = (weights / denominator).astype(jnp.bfloat16)
    context = jnp.einsum(
        "hqk,khd->qhd", softmax_low, split_heads(value_rows), preferred_element_type=jnp.float32
    )
    return (context.reshape(queries.shape), (largest + jnp.log(denominator))[..., 0])


def attend_backward(packed):
    queries, key_rows, value_rows, allowed, log_totals, context_grad = packed
    split_queries = split_heads(queries)
    split_keys = split_heads(key_rows)
    split_values = split_heads(value_rows)
    split_grad = split_heads(context_grad)
    scores = masked_scores(split_queries, split_keys, allowed)
    softmax_out = jnp.exp(scores - log_totals[..., None])
    softmax_low = softmax_out.astype(jnp.bfloat16)
    context = jnp.einsum(
        "hqk,khd->qhd", softmax_low, split_values, preferred_element_type=jnp.float32
    )
    value_grad = jnp.einsum(
        "hqk,qhd->khd", softmax_low, split_grad, preferred_element_type=jnp.float32
    ).astype(jnp.bfloat16)
    prob_grad = jnp.einsum(
        "qhd,khd->hqk", split_grad, split_values, preferred_element_type=jnp.float32
    )
    row_inner = jnp.sum(prob_grad * softmax_out, axis=-1, keepdims=True)
    score_grad = (softmax_out * (prob_grad - row_inner)).astype(jnp.bfloat16)
    query_grad = (
        jnp.einsum("hqk,khd->qhd", score_grad, split_keys, preferred_element_type=jnp.float32)
        * 0.125
    ).astype(jnp.bfloat16)
    key_grad = (
        jnp.einsum("hqk,qhd->khd", score_grad, split_queries, preferred_element_type=jnp.float32)
        * 0.125
    ).astype(jnp.bfloat16)
    row_shape = queries.shape
    return (
        context.reshape(row_shape).astype(jnp.bfloat16),
        query_grad.reshape(row_shape),
        key_grad.reshape(row_shape),
        value_grad.reshape(row_shape),
    )


def split_rows(values, row_count):
    return values.reshape(row_count, values.shape[0] // row_count, values.shape[1])


def project_inputs(inputs_low, inward, inward_pair):
    queries = (product(inputs_low, inward[0]) + inward_pair[0]).astype(jnp.bfloat16)
    key_rows = product(inputs_low, inward[1]).astype(jnp.bfloat16)
    value_rows = (product(inputs_low, inward[2]) + inward_pair[1]).astype(jnp.bfloat16)
    return (queries, key_rows, value_rows)


def layer_forward(current, params, allowed, row_count):
    inward, inward_pair, out_matrix, up_matrix, up_vector, down_matrix, gain_pair, offset_four = (
        params
    )
    token_count = current.shape[0]
    inputs_low = current.astype(jnp.bfloat16)
    queries, key_rows, value_rows = project_inputs(inputs_low, inward, inward_pair)
    context, log_totals = lax.map(
        attend_forward,
        (
            split_rows(queries, row_count),
            split_rows(key_rows, row_count),
            split_rows(value_rows, row_count),
            allowed,
        ),
    )
    context_low = context.reshape(token_count, -1).astype(jnp.bfloat16)
    attention_term = product(context_low, out_matrix)
    mixed_sum = current + lax.psum(attention_term, "tensor") + offset_four[0]
    normed_own = layer_norm(mixed_sum, gain_pair[0], offset_four[2])
    normed_low = normed_own.astype(jnp.bfloat16)
    upward = product(normed_low, up_matrix) + up_vector
    feed_term = product(exact_gelu(upward).astype(jnp.bfloat16), down_matrix)
    second = normed_own + lax.psum(feed_term, "tensor") + offset_four[1]
    outputs_own = layer_norm(second, gain_pair[1], offset_four[3])
    return (outputs_own, outputs_own, (inputs_low, mixed_sum, second, normed_low, log_totals))


def layer_backward(incoming, kept_state, params, allowed, row_count):
    inward, inward_pair, out_matrix, up_matrix, up_vector, down_matrix, gain_pair, offset_four = (
        params
    )
    inputs_low, mixed_sum, second, normed_low, log_totals = kept_state
    token_count = inputs_low.shape[0]
    second_part, gain_two, offset_two = norm_backward(
        incoming, second, gain_pair[1], offset_four[3]
    )
    down_bias_grad = jnp.sum(second_part, axis=0)
    second_low = second_part.astype(jnp.bfloat16)
    upward = product(normed_low, up_matrix) + up_vector
    activated, gelu_pull = jax.vjp(exact_gelu, upward)
    down_grad = contract_rows(activated.astype(jnp.bfloat16), second_low)
    (upward_grad,) = gelu_pull(contract_columns(second_low, down_matrix))
    upward_low = upward_grad.astype(jnp.bfloat16)
    up_grad = contract_rows(normed_low, upward_low)
    up_bias_grad = jnp.sum(upward_low.astype(jnp.float32), axis=0)
    normed_term = contract_columns(upward_low, up_matrix)
    normed_grad = second_part + lax.psum(normed_term, "tensor")
    mixed_part, gain_one, offset_one = norm_backward(
        normed_grad, mixed_sum, gain_pair[0], offset_four[2]
    )
    out_bias_grad = jnp.sum(mixed_part, axis=0)
    mixed_low = mixed_part.astype(jnp.bfloat16)
    queries, key_rows, value_rows = project_inputs(inputs_low, inward, inward_pair)
    context_grad = contract_columns(mixed_low, out_matrix).astype(jnp.bfloat16)
    context_low, query_grad, key_grad, value_grad = lax.map(
        attend_backward,
        (
            split_rows(queries, row_count),
            split_rows(key_rows, row_count),
            split_rows(value_rows, row_count),
            allowed,
            log_totals,
            split_rows(context_grad, row_count),
        ),
    )
    context_low = context_low.reshape(token_count, -1)
    query_grad = query_grad.reshape(token_count, -1)
    key_grad = key_grad.reshape(token_count, -1)
    value_grad = value_grad.reshape(token_count, -1)
    out_grad = contract_rows(context_low, mixed_low)
    inward_grad = jnp.stack(
        [
            contract_rows(inputs_low, query_grad),
            contract_rows(inputs_low, key_grad),
            contract_rows(inputs_low, value_grad),
        ]
    )
    inward_bias_grad = jnp.stack(
        [
            jnp.sum(query_grad.astype(jnp.float32), axis=0),
            jnp.sum(value_grad.astype(jnp.float32), axis=0),
        ]
    ).reshape(2, -1, HEAD_SIZE)
    input_term = (
        contract_columns(query_grad, inward[0])
        + contract_columns(key_grad, inward[1])
        + contract_columns(value_grad, inward[2])
    )
    input_grad = mixed_part + lax.psum(input_term, "tensor")
    gain_grad = jnp.stack([gain_one, gain_two])
    offset_grad = jnp.stack([out_bias_grad, down_bias_grad, offset_one, offset_two])
    layer_grads = (
        inward_grad,
        inward_bias_grad,
        out_grad,
        up_grad,
        up_bias_grad.reshape(-1, 128),
        down_grad,
        gain_grad,
        offset_grad,
    )
    return (input_grad, layer_grads)


def shards(
    frames,
    segment_ids,
    valid_frames,
    inward_weight,
    inward_bias,
    output_weight,
    upward_weight,
    upward_bias,
    downward_weight,
    norm_gains,
    offsets,
    cotangent,
):
    row_count = segment_ids.shape[0]
    allowed = jax.vmap(allowed_mask)(segment_ids, valid_frames)
    layer_count = inward_weight.shape[0]
    layer_index = 0
    layer_params = [
        (
            inward_weight[layer_index],
            inward_bias[layer_index].reshape(2, -1),
            output_weight[layer_index],
            upward_weight[layer_index],
            upward_bias[layer_index].reshape(-1),
            downward_weight[layer_index],
            norm_gains[layer_index],
            offsets[layer_index],
        )
    ]
    current = frames.astype(jnp.float32)
    layer_index = 0
    current, own_rows, kept_state = layer_forward(
        current, layer_params[layer_index], allowed, row_count
    )
    kept_states = [kept_state]
    layer_output = current.astype(jnp.bfloat16)
    incoming = cotangent
    collected = []
    for layer_index in reversed(range(layer_count)):
        incoming, layer_grads = layer_backward(
            incoming, kept_states[layer_index], layer_params[layer_index], allowed, row_count
        )
        collected.append(layer_grads)
    collected = collected[::-1]
    stacked = tuple((jnp.stack([entry[member] for entry in collected]) for member in range(8)))
    reduced = (
        lax.psum_scatter(stacked[0], "dp", scatter_dimension=2, tiled=True),
        lax.psum_scatter(stacked[1], "dp", scatter_dimension=3, tiled=True),
        lax.psum_scatter(stacked[2], "dp", scatter_dimension=2, tiled=True),
        lax.psum_scatter(stacked[3], "dp", scatter_dimension=1, tiled=True),
        lax.psum_scatter(stacked[4], "dp", scatter_dimension=2, tiled=True),
        lax.psum_scatter(stacked[5], "dp", scatter_dimension=2, tiled=True),
        lax.psum_scatter(stacked[6], "dp", scatter_dimension=2, tiled=True),
        lax.psum_scatter(stacked[7], "dp", scatter_dimension=2, tiled=True),
    )
    return (
        layer_output,
        incoming,
        reduced[0],
        reduced[1],
        reduced[2],
        reduced[3],
        reduced[4],
        reduced[5],
        reduced[6],
        reduced[7],
    )


def solution(mesh):
    in_specs = (
        P("dp", None),
        P("dp", None),
        P("dp", None),
        P(None, None, None, "tensor"),
        P(None, None, "tensor", None),
        P(None, "tensor", None),
        P(None, None, "tensor"),
        P(None, "tensor", None),
        P(None, "tensor", None),
        P(),
        P(),
        P("dp", None),
    )
    out_specs = (
        P("dp", None),
        P("dp", None),
        P(None, None, "dp", "tensor"),
        P(None, None, "tensor", "dp"),
        P(None, "tensor", "dp"),
        P(None, "dp", "tensor"),
        P(None, "tensor", "dp"),
        P(None, "tensor", "dp"),
        P(None, None, "dp"),
        P(None, None, "dp"),
    )
    return jax.shard_map(shards, mesh=mesh, in_specs=in_specs, out_specs=out_specs, check_vma=False)
```

profile of v0, /device:TPU:0, one launch (start us, length us, event | category | flops | bytes accessed | tf_op | source)
XLA Modules:
  0.0 1501.4 jit_solution(389023628888043132)
XLA Ops:
  37.7 35.4 %while.28 = (s32[]{:T(128)}, bf16[4,736,192]{1,2,0:T(8,128)(2,1)}, f32[4,3,736]{2,1,0:T(4,128)}, bf16[4,736,192]{1,2,0:T(8,128)(2,1)}, pred[4,736,736]{1,2,0:T(8...) while((s32[]{:T(128)}, bf16[4,736,192]{1,2,0:T(8,128)(2,1)}, ...), condition=%wide.region_3.4_spmd, body=%wide.region_0.3_spmd.sunk | while | flops 435521376 | bytes 25688544 | solution.py:130
  80.8 6.3 fusion.30
  87.9 165.5 %all-reduce.8.cloned.1.call-done = f32[2944,768]{1,0:T(8,128)} async-done(((f32[2944,768]{1,0:T(8,128)}), f32[2944,768]{1,0:T(8,128)}) %all-reduce.8.cloned.1.call-update) | async-done | bytes 9043984 | tf_op jit(solution)/shard_map/psum | solution.py:141
  253.4 9.7 fusion.52
  271.1 24.4 %multiply_convert_fusion.1 = (bf16[2944,768]{1,0:T(8,128)(2,1)S(1)}, f32[2944,768]{1,0:T(8,128)}, f32[2944,768]{1,0:T(8,128)}) fusion(f32[768]{0:T(1024)S(1)} %bitcast_convert_fusion, bf16[2944,768]{1,0:T(8,128)(2,1)S(1)} %fusion.16, bf16[1,768,768]{2,1,0:T(8,128)(2,1)S(1)} %copy-done), kind=kOutput, calls=%fused_computation.48 | convolution fusion | flops 3622109184 | bytes 28314624 | tf_op jit(solution)/shard_map/dot_general | solution.py:14
  297.5 6.0 fusion.21
  303.6 163.7 %all-reduce.10.cloned.1.call-done = f32[2944,768]{1,0:T(8,128)} async-done(((f32[2944,768]{1,0:T(8,128)}), f32[2944,768]{1,0:T(8,128)}) %all-reduce.10.cloned.1.call-update) | async-done | bytes 9043984 | tf_op jit(solution)/shard_map/psum | solution.py:146
  467.3 8.1 fusion.50
  480.7 7.4 fusion.49
  488.1 16.4 %convert_reduce_fusion = (f32[768]{0:T(1024)}, bf16[2944,768]{1,0:T(8,128)(2,1)}) fusion(f32[2944,768]{1,0:T(8,128)} %get-tuple-element.256, bf16[1,768,768]{2,1,0:T(8,128)(2,1)} %param.24, f32[2944,768]{1,0:T(8,128)S(1)} %get-tuple-element.252, f32[2944]{0:T(1024)S(1)} %negate_multiply_fusion.2, f32[2944,768]{1,0:T(8,128)} %get-tuple-element.273, ...), kind=kOutput, calls=%fused_computation.40 | convolution fusion | flops 3515841792 | bytes 32851456 | tf_op jit(solution)/shard_map/dot_general | solution.py:24
  504.5 9.5 fusion.25
  514.2 163.7 %all-reduce.12.cloned.1.call-done = f32[2944,768]{1,0:T(8,128)} async-done(((f32[2944,768]{1,0:T(8,128)}), f32[2944,768]{1,0:T(8,128)}) %all-reduce.12.cloned.1.call-update) | async-done | bytes 9043984 | tf_op jit(solution)/shard_map/psum | solution.py:170
  677.8 15.4 %multiply_reduce_fusion.2 = (f32[768]{0:T(1024)S(1)}, f32[2944]{0:T(1024)S(1)}, f32[768]{0:T(1024)}, f32[2944,768]{1,0:T(8,128)}, f32[768]{0:T(1024)}) fusion(f32[2944,768]{1,0:T(8,128)} %get-tuple-element.258, f32[2944]{0:T(1024)S(1)} %fusion.46, f32[2944]{0:T(1024)S(1)} %broadcast_multiply_fusion.1, f32[768]{0:T(1024)S(1)} %get-tuple-element.209, ...), kind=kLoop, calls=%fused_computation.39 | loop fusion | flops 24865664 | bytes 36235264 | tf_op jit(solution)/shard_map/transpose(jvp())/reduce_sum | solution.py:32
  693.3 12.5 fusion.48
  712.8 73.2 %while.29 = (s32[]{:T(128)}, bf16[4,736,192]{1,2,0:T(8,128)(2,1)}, bf16[4,736,192]{1,2,0:T(8,128)(2,1)}, bf16[4,736,192]{1,2,0:T(8,128)(2,1)}, bf16[4,736,192]{1...) while((s32[]{:T(128)}, bf16[4,736,192]{1,2,0:T(8,128)(2,1)}, ...), condition=%wide.region_17.18_spmd, body=%wide.region_15.17_spmd.sunk | while | flops 1279789952 | bytes 66537612 | solution.py:178
  789.2 6.0 fusion.32
  797.3 6.0 fusion.35
  808.0 11.2 add_add_fusion.2
  822.8 11.2 convolution_bitcast_fusion
  834.1 6.7 copy.73
  848.7 6.2 convolution_bitcast_fusion.2
  878.9 104.0 %all-reduce.14.cloned.1.call-done = f32[2944,768]{1,0:T(8,128)} async-done(((f32[2944,768]{1,0:T(8,128)}), f32[2944,768]{1,0:T(8,128)}) %all-reduce.14.cloned.1.call-update) | async-done | bytes 9043984 | tf_op jit(solution)/shard_map/psum | solution.py:212
  982.9 10.7 add_reduce_fusion
  994.8 9.1 convolution_bitcast_fusion.1
  1005.8 42.4 %reduce-scatter.24.cloned.1.call-done = f32[16,6]{1,0:T(8,128)} async-done(((f32[128,6]{1,0:T(8,128)}), f32[16,6]{1,0:T(8,128)}) %reduce-scatter.24.cloned.1.call-update) | async-done | bytes 400
  1051.1 108.3 %all-reduce.16.cloned.1.call-done = f32[1,768,768]{1,0,2:T(1,128)} async-done(((f32[1,768,768]{1,0,2:T(1,128)}), f32[1,768,768]{1,0,2:T(1,128)}) %all-reduce.16.cloned.1.call-update) | async-done | bytes 2359312
  1161.8 19.6 %all-reduce = f32[1,2,3,64]{3,2,1,0:T(4,128)S(1)} all-reduce(f32[1,2,3,64]{3,2,1,0:T(4,128)S(1)} %pad_maximum_fusion), channel_id=3, replica_groups=mesh['dp'=8,'tensor'=4] {'dp'}, use_global_device_ids=true, to_apply=%region_22.23.clone | all-reduce | flops 384 | bytes 3072
  1182.0 41.5 %reduce-scatter.26.cloned.1.call-done = f32[96,2]{1,0:T(8,128)} async-done(((f32[768,2]{1,0:T(8,128)}), f32[96,2]{1,0:T(8,128)}) %reduce-scatter.26.cloned.1.call-update) | async-done | bytes 784
  1225.0 63.8 %reduce-scatter.22.cloned.1.call-done = f32[96,192]{1,0:T(8,128)} async-done(((f32[768,192]{1,0:T(8,128)}), f32[96,192]{1,0:T(8,128)}) %reduce-scatter.22.cloned.1.call-update) | async-done | bytes 73744
  1290.5 67.4 %reduce-scatter.20.cloned.1.call-done = f32[96,576]{1,0:T(8,128)} async-done(((f32[768,576]{1,0:T(8,128)}), f32[96,576]{1,0:T(8,128)}) %reduce-scatter.20.cloned.1.call-update) | async-done | bytes 221200
  1359.8 61.9 %reduce-scatter.28.cloned.1.call-done = f32[96,4]{1,0:T(8,128)} async-done(((f32[768,4]{1,0:T(8,128)}), f32[96,4]{1,0:T(8,128)}) %reduce-scatter.28.cloned.1.call-update) | async-done | bytes 1552
  1423.2 71.2 %reduce-scatter.18.cloned.1.call-done = f32[1,96,768]{2,1,0:T(8,128)} async-done(((f32[1,768,768]{2,1,0:T(8,128)}), f32[1,96,768]{2,1,0:T(8,128)}) %reduce-scatter.18.cloned.1.call-update) | async-done | bytes 294928 | tf_op jit(solution)/shard_map/reduce_scatter | solution.py:278
  (265 shorter events, 228.6 us)
Async XLA Ops:
  7.2 263.9 %copy-start = (bf16[1,768,768]{2,1,0:T(8,128)(2,1)S(1)}, bf16[1,768,768]{2,1,0:T(8,128)(2,1)}, u32[]{:S(2)}) copy-start(bf16[1,768,768]{2,1,0:T(8,128)(2,1)} %param.22) | copy-start | bytes 3538948
  7.2 246.2 %all-reduce.8.cloned.1.call-start = ((), (), s32[]{:S(2)}) async-start(), calls=%async_computation.6 | async-start | bytes 18087936 | tf_op jit(solution)/shard_map/psum | solution.py:141
  26.8 7.3 copy-start.20
  26.8 7.3 copy-start.14
  73.1 14.0 copy-start.4
  87.1 380.2 %all-reduce.10.cloned.1.call-start = ((), (), s32[]{:S(2)}) async-start(), calls=%async_computation.7 | async-start | bytes 18087936 | tf_op jit(solution)/shard_map/psum | solution.py:146
  263.1 6.1 copy-start.2
  271.0 24.4 %copy-start.9 = (bf16[2944,768]{1,0:T(8,128)(2,1)}, bf16[2944,768]{1,0:T(8,128)(2,1)S(1)}, u32[]{:S(2)}) copy-start(bf16[2944,768]{1,0:T(8,128)(2,1)S(1)} %fusion.16) | copy-start | bytes 13565956
  271.0 26.5 %copy-start.24 = (bf16[1,768,768]{2,1,0:T(8,128)(2,1)S(1)}, bf16[1,768,768]{2,1,0:T(8,128)(2,1)}, u32[]{:S(2)}) copy-start(bf16[1,768,768]{2,1,0:T(8,128)(2,1)} %param.24) | copy-start | bytes 3538948
  303.5 374.3 %all-reduce.12.cloned.1.call-start = ((), (), s32[]{:S(2)}) async-start(), calls=%async_computation.8 | async-start | bytes 18087936 | tf_op jit(solution)/shard_map/psum | solution.py:170
  467.3 9.3 slice-start.2
  467.3 9.3 slice-start.3
  467.3 9.3 slice-start.4
  488.1 16.4 %copy-start.3 = (f32[2944,768]{1,0:T(8,128)}, f32[2944,768]{1,0:T(8,128)S(1)}, u32[]{:S(2)}) copy-start(f32[2944,768]{1,0:T(8,128)S(1)} %get-tuple-element.252) | copy-start | bytes 27131908
  488.1 189.7 %copy-start.12 = (f32[2944]{0:T(1024)}, f32[2944]{0:T(1024)S(1)}, u32[]{:S(2)}) copy-start(f32[2944]{0:T(1024)S(1)} %negate_multiply_fusion.2) | copy-start | bytes 35332
  514.1 468.9 %all-reduce.14.cloned.1.call-start = ((), (), s32[]{:S(2)}) async-start(), calls=%async_computation.9 | async-start | bytes 18087936 | tf_op jit(solution)/shard_map/psum | solution.py:212
  693.3 12.5 copy-start.11
  819.2 229.0 %reduce-scatter.24.cloned.1.call-start = ((), (), s32[]{:S(2)}) async-start(), calls=%async_computation.13 | async-start | bytes 73728
  822.8 336.7 %all-reduce.16.cloned.1.call-start = ((), (), s32[]{:S(2)}) async-start(), calls=%async_computation.16 | async-start | bytes 4718592
  834.1 6.8 copy-start.18
  840.8 382.8 %reduce-scatter.26.cloned.1.call-start = ((), (), s32[]{:S(2)}) async-start(), calls=%async_computation.14 | async-start | bytes 442368
  848.6 440.1 %reduce-scatter.22.cloned.1.call-start = ((), (), s32[]{:S(2)}) async-start(), calls=%async_computation.12 | async-start | bytes 884736
  860.4 497.5 %reduce-scatter.20.cloned.1.call-start = ((), (), s32[]{:S(2)}) async-start(), calls=%async_computation.11 | async-start | bytes 2211840
  871.3 7.6 copy-start.15
  871.3 7.6 copy-start.17
  871.3 7.6 copy-start.16
  878.8 542.9 %reduce-scatter.28.cloned.1.call-start = ((), (), s32[]{:S(2)}) async-start(), calls=%async_computation.15 | async-start | bytes 442368
  994.7 9.2 copy-start.25
  994.7 166.5 %copy-start.6 = (bf16[4,736,192]{1,2,0:T(8,128)(2,1)S(1)}, bf16[4,736,192]{1,2,0:T(8,128)(2,1)}, u32[]{:S(2)}) copy-start(bf16[4,736,192]{1,2,0:T(8,128)(2,1)} %get-tuple-element.110) | copy-start | bytes 3391492
  994.7 166.5 %copy-start.8 = (bf16[4,736,192]{1,2,0:T(8,128)(2,1)S(1)}, bf16[4,736,192]{1,2,0:T(8,128)(2,1)}, u32[]{:S(2)}) copy-start(bf16[4,736,192]{1,2,0:T(8,128)(2,1)} %get-tuple-element.112) | copy-start | bytes 3391492
  994.7 499.7 %reduce-scatter.18.cloned.1.call-start = ((), (), s32[]{:S(2)}) async-start(), calls=%async_computation.10 | async-start | bytes 2654208 | tf_op jit(solution)/shard_map/reduce_scatter | solution.py:278
  994.8 499.6 %copy-start.1 = (bf16[1,768,768]{2,1,0:T(8,128)(2,1)S(1)}, bf16[1,768,768]{2,1,0:T(8,128)(2,1)}, u32[]{:S(2)}) copy-start(bf16[1,768,768]{2,1,0:T(8,128)(2,1)} %param.22) | copy-start | bytes 3538948
  (10 other events, 30.8 us)
Sparse Core Ops, SparseCore 0:
  87.3 166.1 all-reduce.7
  303.7 163.5 all-reduce.9
  514.2 163.5 all-reduce.11
  819.3 163.5 all-reduce.13
  986.8 61.4 reduce-scatter.23
  1051.6 107.7 all-reduce.15
  1163.1 60.4 reduce-scatter.25
  1227.2 61.5 reduce-scatter.21
  1292.3 65.5 reduce-scatter.19
  1361.3 60.3 reduce-scatter.27
  1426.2 68.1 reduce-scatter.17
where the time goes:
time: 1510 us; the launch traced here: 1500 us
  waiting for transfers between devices  1050 us (70%)
  matrix products  195 us (13%)
  local copies, waits for them, and re-layouts  118 us (8%)
  other arithmetic  98.1 us (6%)
  blocking collectives  19.6 us (1%)
  between operations  16.2 us (1%)
    unnamed x17, waiting for transfers between devices  386 us
    psum x1, waiting for transfers between devices, layer_forward(): mixed_sum = current + lax.psum(attention_term, 'tensor') + offset_four[0]  166 us
    psum x1, waiting for transfers between devices, layer_forward(): second = normed_own + lax.psum(feed_term, 'tensor') + offset_four[1]  164 us
    psum x1, waiting for transfers between devices, layer_backward(): normed_grad = second_part + lax.psum(normed_term, 'tensor')  164 us
    psum x1, waiting for transfers between devices, layer_backward(): input_grad = mixed_part + lax.psum(input_term, 'tensor')  104 us
    reduce_scatter x1, waiting for transfers between devices, shards(): lax.psum_scatter(stacked[3], 'dp', scatter_dimension=1, tiled=True)  71.2 us
    dot_general x6, matrix products, contract_columns(): lax.dot_general(left_side, right_side, (((1,), (1,)), ((), ())), preferre...  54.2 us
    dot_general x6, matrix products, product(): return jnp.dot(left_side, right_side, preferred_element_type=jnp.float32)  49.4 us
  transfers between devices with their start and end apart: 11, of which 11 were waited for; matrix products, arithmetic and copies ran while one was open for 6% of the time, Pallas kernels for 0%

commit v1 on v0

--- a/solution.py
+++ b/solution.py
@@ -138,12 +138,12 @@
     )
     context_low = context.reshape(token_count, -1).astype(jnp.bfloat16)
     attention_term = product(context_low, out_matrix)
-    mixed_sum = current + lax.psum(attention_term, "tensor") + offset_four[0]
+    mixed_sum = current + attention_term + offset_four[0]
     normed_own = layer_norm(mixed_sum, gain_pair[0], offset_four[2])
     normed_low = normed_own.astype(jnp.bfloat16)
     upward = product(normed_low, up_matrix) + up_vector
     feed_term = product(exact_gelu(upward).astype(jnp.bfloat16), down_matrix)
-    second = normed_own + lax.psum(feed_term, "tensor") + offset_four[1]
+    second = normed_own + feed_term + offset_four[1]
     outputs_own = layer_norm(second, gain_pair[1], offset_four[3])
     return (outputs_own, outputs_own, (inputs_low, mixed_sum, second, normed_low, log_totals))
 
@@ -167,7 +167,7 @@
     up_grad = contract_rows(normed_low, upward_low)
     up_bias_grad = jnp.sum(upward_low.astype(jnp.float32), axis=0)
     normed_term = contract_columns(upward_low, up_matrix)
-    normed_grad = second_part + lax.psum(normed_term, "tensor")
+    normed_grad = second_part + normed_term
     mixed_part, gain_one, offset_one = norm_backward(
         normed_grad, mixed_sum, gain_pair[0], offset_four[2]
     )
@@ -209,7 +209,7 @@
         + contract_columns(key_grad, inward[1])
         + contract_columns(value_grad, inward[2])
     )
-    input_grad = mixed_part + lax.psum(input_term, "tensor")
+    input_grad = mixed_part + input_term
     gain_grad = jnp.stack([gain_one, gain_two])
     offset_grad = jnp.stack([out_bias_grad, down_bias_grad, offset_one, offset_two])
     layer_grads = (
@@ -240,58 +240,57 @@
     cotangent,
 ):
     row_count = segment_ids.shape[0]
-    allowed = jax.vmap(allowed_mask)(segment_ids, valid_frames)
-    layer_count = inward_weight.shape[0]
-    layer_index = 0
-    layer_params = [
-        (
-            inward_weight[layer_index],
-            inward_bias[layer_index].reshape(2, -1),
-            output_weight[layer_index],
-            upward_weight[layer_index],
-            upward_bias[layer_index].reshape(-1),
-            downward_weight[layer_index],
-            norm_gains[layer_index],
-            offsets[layer_index],
-        )
-    ]
-    current = frames.astype(jnp.float32)
-    layer_index = 0
-    current, own_rows, kept_state = layer_forward(
-        current, layer_params[layer_index], allowed, row_count
-    )
-    kept_states = [kept_state]
-    layer_output = current.astype(jnp.bfloat16)
-    incoming = cotangent
-    collected = []
-    for layer_index in reversed(range(layer_count)):
-        incoming, layer_grads = layer_backward(
-            incoming, kept_states[layer_index], layer_params[layer_index], allowed, row_count
-        )
-        collected.append(layer_grads)
-    collected = collected[::-1]
-    stacked = tuple((jnp.stack([entry[member] for entry in collected]) for member in range(8)))
-    reduced = (
-        lax.psum_scatter(stacked[0], "dp", scatter_dimension=2, tiled=True),
-        lax.psum_scatter(stacked[1], "dp", scatter_dimension=3, tiled=True),
-        lax.psum_scatter(stacked[2], "dp", scatter_dimension=2, tiled=True),
-        lax.psum_scatter(stacked[3], "dp", scatter_dimension=1, tiled=True),
-        lax.psum_scatter(stacked[4], "dp", scatter_dimension=2, tiled=True),
-        lax.psum_scatter(stacked[5], "dp", scatter_dimension=2, tiled=True),
-        lax.psum_scatter(stacked[6], "dp", scatter_dimension=2, tiled=True),
-        lax.psum_scatter(stacked[7], "dp", scatter_dimension=2, tiled=True),
-    )
+    part_count = lax.axis_size("tensor")
+    own_rows = row_count // part_count
+    token_count = frames.shape[0] // part_count
+    place = lax.axis_index("tensor")
+
+    def own(values, count):
+        return lax.dynamic_slice_in_dim(values, place * count, count, 0)
+
+    def whole(values, axis):
+        return lax.all_gather(values, "tensor", axis=axis, tiled=True)
+
+    allowed = jax.vmap(allowed_mask)(own(segment_ids, own_rows), own(valid_frames, own_rows))
+    params = (
+        whole(inward_weight[0], 2),
+        whole(inward_bias[0], 1).reshape(2, -1),
+        whole(output_weight[0], 0),
+        whole(upward_weight[0], 1),
+        whole(upward_bias[0], 0).reshape(-1),
+        whole(downward_weight[0], 0),
+        norm_gains[0],
+        offsets[0],
+    )
+    current = own(frames, token_count).astype(jnp.float32)
+    current, _, kept_state = layer_forward(current, params, allowed, own_rows)
+    layer_output = whole(current.astype(jnp.bfloat16), 0)
+    incoming, grads = layer_backward(
+        own(cotangent, token_count), kept_state, params, allowed, own_rows
+    )
+    grad_frames = whole(incoming.astype(jnp.bfloat16), 0).astype(jnp.float32)
+
+    def scatter(values, tensor_dim, dp_dim, low=True):
+        if low:
+            values = values.astype(jnp.bfloat16)
+        if tensor_dim is None:
+            values = lax.psum(values, "tensor")
+        else:
+            values = lax.psum_scatter(values, "tensor", scatter_dimension=tensor_dim, tiled=True)
+        values = lax.psum_scatter(values, "dp", scatter_dimension=dp_dim, tiled=True)
+        return values.astype(jnp.float32)[None]
+
     return (
         layer_output,
-        incoming,
-        reduced[0],
-        reduced[1],
-        reduced[2],
-        reduced[3],
-        reduced[4],
-        reduced[5],
-        reduced[6],
-        reduced[7],
+        grad_frames,
+        scatter(grads[0], 2, 1),
+        scatter(grads[1], 1, 2, False),
+        scatter(grads[2], 0, 1),
+        scatter(grads[3], 1, 0),
+        scatter(grads[4], 0, 1, False),
+        scatter(grads[5], 0, 1),
+        scatter(grads[6], None, 1, False),
+        scatter(grads[7], None, 1, False),
     )
 
 

time: 1510 us -> 946 us (0.63)
  waiting for transfers between devices: 1050 us -> 565 us
  local copies, waits for them, and re-layouts: 118 us -> 45.4 us
  other arithmetic: 98.1 us -> 58.9 us
  blocking collectives: 19.6 us -> 43.7 us
    psum x4 -> x0, waiting for transfers between devices: 597 us -> none  [the longest x1 166 us: layer_forward(): mixed_sum = current + lax.psum(attention_term, 'tensor') + offset_four[0]]
    reduce_scatter x1 -> x5, waiting for transfers between devices: 71.2 us -> 237 us  [the longest x2 132 us: scatter(): lax.psum_scatter(values, 'dp', scatter_dimension=dp_dim, tiled=True)]
    unnamed x17 -> x23, waiting for transfers between devices: 386 us -> 243 us
    all_gather x0 -> x6, waiting for transfers between devices: none -> 85 us  [whole(): return lax.all_gather(values, 'tensor', axis=axis, tiled=True)]
    reduce_sum x4 -> x2, other arithmetic: 37.7 us -> 4.47 us  [layer_norm(): centred = values - jnp.mean(values, axis=-1, keepdims=True)]
    dot_general x6, matrix products: 54.2 us -> 33.9 us  [contract_columns(): lax.dot_general(left_side, right_side, (((1,), (1,)), ((), ())), preferre...]
    dynamic_slice x24 -> x1, local copies, waits for them, and re-layouts: 20.2 us -> 0.02 us  [own(): return lax.dynamic_slice_in_dim(values, place * count, count, 0)]
    reshape x8 -> x0, local copies, waits for them, and re-layouts: 18.9 us -> none  [the longest x4 10.6 us: split_rows(): values.reshape(row_count, values.shape[0] // row_count, values.shape[1])]
  transfers between devices with their start and end apart: 11 -> 17, of which waited for: 11 -> 14; matrix products, arithmetic and copies ran while one was open for 6% -> 23% of each run, Pallas kernels for 0% -> 0%
where the time goes in v1:
time: 946 us; the launch traced here: 936 us
  waiting for transfers between devices  565 us (60%)
  matrix products  204 us (22%)
  other arithmetic  58.9 us (6%)
  local copies, waits for them, and re-layouts  45.4 us (5%)
  blocking collectives  43.7 us (5%)
  between operations  17.2 us (2%)
    unnamed x23, waiting for transfers between devices  243 us
    reduce_scatter x2, waiting for transfers between devices, scatter(): lax.psum_scatter(values, 'dp', scatter_dimension=dp_dim, tiled=True)  132 us
    reduce_scatter x3, waiting for transfers between devices, scatter(): lax.psum_scatter(values, 'tensor', scatter_dimension=tensor_dim, tiled=True)  105 us
    all_gather x6, waiting for transfers between devices, whole(): return lax.all_gather(values, 'tensor', axis=axis, tiled=True)  85 us
    dot_general x6, matrix products, product(): return jnp.dot(left_side, right_side, preferred_element_type=jnp.float32)  48.5 us
    unnamed x122, local copies, waits for them, and re-layouts  38.2 us
    dot_general x6, matrix products, contract_columns(): lax.dot_general(left_side, right_side, (((1,), (1,)), ((), ())), preferre...  33.9 us
    unnamed x2, blocking collectives  32.2 us
  transfers between devices with their start and end apart: 17, of which 14 were waited for; matrix products, arithmetic and copies ran while one was open for 23% of the time, Pallas kernels for 0%

profile of v1, /device:TPU:0, one launch (start us, length us, event | category | flops | bytes accessed | tf_op | source)
XLA Modules:
  0.0 936.5 jit_solution(14709448394391731560)
XLA Ops:
  25.7 17.5 %all-gather.17.cloned.1.call-done = bf16[1,3,768,768]{2,3,1,0:T(8,128)(2,1)} async-done(((bf16[1,3,768,192]{2,3,1,0:T(8,128)(2,1)}), bf16[1,3,768,768]{2,3,1,0:T(8,128)(2,1)}) %all-gather.17.cloned.1.call-update) | async-done | bytes 3538960 | tf_op jit(solution)/shard_map/all_gather | solution.py:252
  56.1 12.5 %fusion.65 = (f32[12,736]{1,0:T(8,128)S(1)}, f32[12,736,736]{1,2,0:T(8,128)}) fusion(bf16[736,12,64]{0,2,1:T(8,128)(2,1)S(1)} %bitcast.136, bf16[736,12,64]{0,2,1:T(8,128)(2,1)S(1)} %bitcast.133, pred[736,736]{0,1:T(8,128)(4,1)} %fusion.24), kind=kOutput, calls=%fused_computation.135 | convolution fusion | flops 851537280 | bytes 28839424 | tf_op jit(solution)/shard_map/while/body/eval_jaxpr/qhd,khd->hqk/dot_general | solution.py:56
  68.6 12.2 %fusion = f32[12,736]{1,0:T(8,128)S(1)} fusion(f32[12,736,736]{1,2,0:T(8,128)} %get-tuple-element.120, f32[12,736]{1,0:T(8,128)S(1)} %get-tuple-element.119), kind=kLoop, calls=%fused_computation.6 | loop fusion | flops 12991872 | bytes 26072064 | tf_op jit(solution)/shard_map/while/body/eval_jaxpr/reduce_sum | solution.py:67
  80.8 12.7 %fusion.32 = bf16[12,64,736]{2,1,0:T(8,128)(2,1)} fusion(bf16[736,12,64]{0,2,1:T(8,128)(2,1)S(1)} %bitcast.139, f32[12,736,736]{1,2,0:T(8,128)} %get-tuple-element.120, f32[12,736]{1,0:T(8,128)S(1)} %fusion, f32[12,736]{1,0:T(8,128)S(1)} %get-tuple-element.119), kind=kOutput, calls=%fused_computation.75 | convolution fusion | flops 852111360 | bytes 28333056 | tf_op jit(solution)/shard_map/while/body/eval_jaxpr/hqk,khd->qhd/dot_general | solution.py:69
  97.4 14.5 %fusion.29 = bf16[12,64,736]{2,1,0:T(8,128)(2,1)} fusion(bf16[736,12,64]{0,2,1:T(8,128)(2,1)S(1)} %bitcast.140, f32[12,736,736]{1,2,0:T(8,128)} %get-tuple-element.120, f32[12,736]{1,0:T(8,128)S(1)} %log_add_fusion), kind=kOutput, calls=%fused_computation.70 | convolution fusion | flops 845611008 | bytes 28297728 | tf_op jit(solution)/shard_map/while/body/eval_jaxpr/hqk,khd->qhd/dot_general | solution.py:84
  111.9 27.5 %multiply_convert_fusion.1 = (bf16[736,3072]{1,0:T(8,128)(2,1)}, f32[736,3072]{1,0:T(8,128)}, f32[736,3072]{1,0:T(8,128)}) fusion(f32[3072]{0:T(1024)S(1)} %bitcast.165, bf16[1,768,3072]{2,1,0:T(8,128)(2,1)} %all-gather.21.cloned.1.call-done, f32[736,768]{1,0:T(8,128)S(1)} %get-tuple-element.122, f32[768]{0:T(1024)S(1)} %copy-done.34, ...), kind=kOutput, calls=%fused_computation.13 | convolution fusion | flops 3624935424 | bytes 29613824 | tf_op jit(solution)/shard_map/dot_general | solution.py:14
  140.2 7.8 fusion.67
  153.0 12.5 %convert_reduce_fusion = (f32[3072]{0:T(1024)}, bf16[736,3072]{1,0:T(8,128)(2,1)}) fusion(f32[736,3072]{1,0:T(8,128)} %get-tuple-element.117, bf16[1,3072,768]{2,1,0:T(8,128)(2,1)S(1)} %bitcast.170, f32[736,768]{1,0:T(8,128)S(1)} %get-tuple-element.115, f32[736]{0:T(1024)S(1)} %negate_multiply_fusion.2, f32[736,3072]{1,0:T(8,128)} %get-tuple-element.123, ...), kind=kOutput, calls=%fused_computation.11 | convolution fusion | flops 3512448000 | bytes 29617024 | tf_op jit(solution)/shard_map/dot_general | solution.py:24
  165.5 8.7 multiply_reduce_fusion.2
  182.5 13.0 %convert_reduce_fusion.1 = (f32[12,64]{1,0:T(8,128)}, bf16[12,64,736]{2,1,0:T(8,128)(2,1)}) fusion(bf16[736,12,64]{0,2,1:T(8,128)(2,1)} %bitcast.142, f32[12,736,736]{1,2,0:T(8,128)} %get-tuple-element.120, f32[12,736]{1,0:T(8,128)S(1)} %log_add_fusion), kind=kOutput, calls=%fused_computation.42 | convolution fusion | flops 846740736 | bytes 28300800 | tf_op jit(solution)/shard_map/while/body/eval_jaxpr/hqk,qhd->khd/dot_general | solution.py:87
  195.4 21.4 %multiply_reduce_fusion = (f32[12,736]{1,0:T(8,128)}, f32[12,736,736]{1,2,0:T(8,128)}) fusion(f32[12,736,736]{1,2,0:T(8,128)} %get-tuple-element.120, f32[12,736]{1,0:T(8,128)S(1)} %log_add_fusion, bf16[736,12,64]{0,2,1:T(8,128)(2,1)} %bitcast.143, bf16[736,12,64]{0,2,1:T(8,128)(2,1)S(1)} %bitcast.141), kind=kOutput, calls=%fused_computation.1 | convolution fusion | flops 851537280 | bytes 54334464 | tf_op jit(solution)/shard_map/while/body/eval_jaxpr/qhd,khd->hqk/dot_general | solution.py:90
  226.5 22.9 %multiply_convert_fusion = bf16[12,736,736]{1,2,0:T(8,128)(2,1)} fusion(f32[12,736,736]{1,2,0:T(8,128)} %get-tuple-element.128, f32[12,736,736]{1,2,0:T(8,128)} %get-tuple-element.120, f32[12,736]{1,0:T(8,128)S(1)} %copy-done.15, f32[12,736]{1,0:T(8,128)S(1)} %copy-done.12), kind=kLoop, calls=%fused_computation | loop fusion | flops 26001408 | bytes 65074176 | tf_op jit(solution)/shard_map/while/body/eval_jaxpr/convert_element_type | solution.py:94
  249.4 8.9 multiply_convert_fusion.2
  261.2 7.5 convert_reduce_fusion.2
  273.6 8.1 copy.67
  287.2 9.1 convolution_convert_fusion
  297.0 9.4 %convolution_convert_fusion.1 = bf16[768,3072]{1,0:T(8,128)(2,1)} fusion(bf16[736,3072]{1,0:T(8,128)(2,1)} %get-tuple-element.134, f32[736,768]{1,0:T(8,128)} %copy-done.6, f32[768]{0:T(1024)S(1)} %copy-done.35, f32[768]{0:T(1024)S(1)} %copy-done.27, f32[736]{0:T(1024)S(1)} %copy-done.29, f32[736]{0:T(1024)S(1)} %copy-done.17), kind=kOutput, calls=%fused_computation.28 | convolution fusion | flops 3478069248 | bytes 11513600 | tf_op jit(solution)/shard_map/dot_general | solution.py:18
  309.3 37.4 %reduce-scatter.45.cloned.1.call-done = f32[96,4]{1,0:T(8,128)} async-done(((f32[768,4]{1,0:T(8,128)}), f32[96,4]{1,0:T(8,128)}) %reduce-scatter.45.cloned.1.call-update) | async-done | bytes 1552
  347.6 10.9 %all-reduce.3 = (f32[2,12,64]{2,0,1:T(2,128)S(1)}, f32[24,128]{1,0:T(8,128)S(1)}, f32[2,96]{1,0:T(2,128)}, f32[4,96]{1,0:T(4,128)}) all-reduce(f32[2,12,64]{2,0,1:T(2,128)S(1)} %pad_maximum_fusion.1, f32[24,128]{1,0:T(8,128)S(1)} %bitcast.164, f32[2,96]{1,0:T(2,128)S(1)} %copy.78, ...), channel_id=10, replica_groups=mesh['dp'=8,'tensor'=4] {'tensor'}, use_global_device_ids=true, to_apply=%region_15.16.clone | all-reduce | flops 5184 | bytes 41472
  363.4 10.7 %reduce-scatter.27.cloned.1.call-done = bf16[192,768]{1,0:T(8,128)(2,1)} async-done(((bf16[768,768]{1,0:T(8,128)(2,1)}), bf16[192,768]{1,0:T(8,128)(2,1)}) %reduce-scatter.27.cloned.1.call-update) | async-done | bytes 294928 | tf_op jit(solution)/shard_map/reduce_scatter | solution.py:279
  383.5 33.7 %reduce-scatter.35.cloned.1.call-done = bf16[192,2304]{1,0:T(8,128)(2,1)} async-done(((bf16[768,2304]{1,0:T(8,128)(2,1)}), bf16[192,2304]{1,0:T(8,128)(2,1)}) %reduce-scatter.35.cloned.1.call-update) | async-done | bytes 884752
  421.6 46.1 %reduce-scatter.33.cloned.1.call-done = bf16[768,768]{1,0:T(8,128)(2,1)} async-done(((bf16[3072,768]{1,0:T(8,128)(2,1)}), bf16[768,768]{1,0:T(8,128)(2,1)}) %reduce-scatter.33.cloned.1.call-update) | async-done | bytes 1179664 | tf_op jit(solution)/shard_map/reduce_scatter | solution.py:279
  470.1 48.6 %reduce-scatter.29.cloned.1.call-done = bf16[768,768]{1,0:T(8,128)(2,1)} async-done(((bf16[768,3072]{1,0:T(8,128)(2,1)}), bf16[768,768]{1,0:T(8,128)(2,1)}) %reduce-scatter.29.cloned.1.call-update) | async-done | bytes 1179664 | tf_op jit(solution)/shard_map/reduce_scatter | solution.py:279
  520.7 21.4 %all-reduce.1 = f32[2,3,64]{2,0,1:T(2,128)S(1)} all-reduce(f32[2,3,64]{2,0,1:T(2,128)S(1)} %constant_dynamic-slice_fusion.1), channel_id=11, replica_groups=mesh['dp'=8,'tensor'=4] {'dp'}, use_global_device_ids=true, to_apply=%region_16.17.clone | all-reduce | flops 384 | bytes 3072
  542.7 41.3 %reduce-scatter.39.cloned.1.call-done = f32[16,6]{1,0:T(8,128)} async-done(((f32[128,6]{1,0:T(8,128)}), f32[16,6]{1,0:T(8,128)}) %reduce-scatter.39.cloned.1.call-update) | async-done | bytes 400
  585.3 62.2 %reduce-scatter.37.cloned.1.call-done = bf16[96,192]{1,0:T(8,128)(2,1)} async-done(((bf16[768,192]{1,0:T(8,128)(2,1)}), bf16[96,192]{1,0:T(8,128)(2,1)}) %reduce-scatter.37.cloned.1.call-update) | async-done | bytes 36880
  649.1 35.4 %all-gather.15.cloned.1.call-done = bf16[2944,768]{1,0:T(8,128)(2,1)} async-done(((bf16[736,768]{1,0:T(8,128)(2,1)}), bf16[2944,768]{1,0:T(8,128)(2,1)}) %all-gather.15.cloned.1.call-update) | async-done | bytes 4522000 | tf_op jit(solution)/shard_map/all_gather | solution.py:252
  684.5 6.6 convert_element_type.185
  691.1 31.2 %all-gather.13.cloned.1.call-done = bf16[2944,768]{1,0:T(8,128)(2,1)} async-done(((bf16[736,768]{1,0:T(8,128)(2,1)}), bf16[2944,768]{1,0:T(8,128)(2,1)}) %all-gather.13.cloned.1.call-update) | async-done | bytes 4522000 | tf_op jit(solution)/shard_map/all_gather | solution.py:252
  722.3 67.9 %reduce-scatter.25.cloned.1.call-done = bf16[3,96,192]{2,1,0:T(8,128)(2,1)} async-done(((bf16[3,768,192]{2,1,0:T(8,128)(2,1)}), bf16[3,96,192]{2,1,0:T(8,128)(2,1)}) %reduce-scatter.25.cloned.1.call-update) | async-done | bytes 110608 | tf_op jit(solution)/shard_map/reduce_scatter | solution.py:280
  791.8 65.0 %reduce-scatter.41.cloned.1.call-done = bf16[96,768]{1,0:T(8,128)(2,1)} async-done(((bf16[768,768]{1,0:T(8,128)(2,1)}), bf16[96,768]{1,0:T(8,128)(2,1)}) %reduce-scatter.41.cloned.1.call-update) | async-done | bytes 147472
  858.9 64.2 %reduce-scatter.31.cloned.1.call-done = bf16[96,768]{1,0:T(8,128)(2,1)} async-done(((bf16[768,768]{1,0:T(8,128)(2,1)}), bf16[96,768]{1,0:T(8,128)(2,1)}) %reduce-scatter.31.cloned.1.call-update) | async-done | bytes 147472 | tf_op jit(solution)/shard_map/reduce_scatter | solution.py:280
  (221 shorter events, 110.5 us)
Async XLA Ops:
  7.2 11.1 %copy-start.40 = (bf16[1,6,128]{2,1,0:T(8,128)(2,1)S(1)}, bf16[1,6,128]{2,1,0:T(8,128)(2,1)}, u32[]{:S(2)}) copy-start(bf16[1,6,128]{2,1,0:T(8,128)(2,1)} %param.19) | copy-start | bytes 4612
  7.2 35.9 %all-gather.17.cloned.1.call-start = ((), (), s32[]{:S(2)}) async-start(), calls=%async_computation.18 | async-start | bytes 4423680 | tf_op jit(solution)/shard_map/all_gather | solution.py:252
  8.0 85.6 %all-gather.19.cloned.1.call-start = ((), (), s32[]{:S(2)}) async-start(), calls=%async_computation.19 | async-start | bytes 1474560 | tf_op jit(solution)/shard_map/all_gather | solution.py:252
  8.7 103.2 %all-gather.21.cloned.1.call-start = ((), (), s32[]{:S(2)}) async-start(), calls=%async_computation.20 | async-start | bytes 5898240 | tf_op jit(solution)/shard_map/all_gather | solution.py:252
  9.5 130.8 %all-gather.23.cloned.1.call-start = ((), (), s32[]{:S(2)}) async-start(), calls=%async_computation.21 | async-start | bytes 5898240 | tf_op jit(solution)/shard_map/all_gather | solution.py:252
  10.0 298.4 %reduce-scatter.43.cloned.1.call-start = ((), (), s32[]{:S(2)}) async-start(), calls=%async_computation.26 | async-start | bytes 442368
  80.8 114.6 %copy-start.11 = (f32[12,736]{1,0:T(8,128)}, f32[12,736]{1,0:T(8,128)S(1)}, u32[]{:S(2)}) copy-start(f32[12,736]{1,0:T(8,128)S(1)} %log_add_fusion) | copy-start | bytes 105988
  80.8 12.8 %copy-start.37 = (f32[768]{0:T(1024)S(1)}, f32[768]{0:T(1024)}, u32[]{:S(2)}) copy-start(f32[768]{0:T(1024)} %get-tuple-element.102) | copy-start | bytes 9220
  96.9 68.6 %copy-start.6 = (f32[736,768]{1,0:T(8,128)}, f32[736,768]{1,0:T(8,128)S(1)}, u32[]{:S(2)}) copy-start(f32[736,768]{1,0:T(8,128)S(1)} %get-tuple-element.122) | copy-start | bytes 6782980
  96.9 77.3 %copy-start.16 = (f32[736]{0:T(1024)}, f32[736]{0:T(1024)S(1)}, u32[]{:S(2)}) copy-start(f32[736]{0:T(1024)S(1)} %broadcast_multiply_fusion.1) | copy-start | bytes 8836
  97.3 76.9 %copy-start.28 = (f32[736]{0:T(1024)}, f32[736]{0:T(1024)S(1)}, u32[]{:S(2)}) copy-start(f32[736]{0:T(1024)S(1)} %fusion.52) | copy-start | bytes 8836
  97.3 14.6 %copy-start.26 = (f32[768]{0:T(1024)S(1)}, f32[768]{0:T(1024)}, u32[]{:S(2)}) copy-start(f32[768]{0:T(1024)} %get-tuple-element.105) | copy-start | bytes 9220
  97.3 14.6 %copy-start.32 = (f32[1,24,128]{2,0,1:T(1,128)S(1)}, f32[1,24,128]{2,0,1:T(1,128)}, u32[]{:S(2)}) copy-start(f32[1,24,128]{2,0,1:T(1,128)} %convert_element_type.198) | copy-start | bytes 36868
  97.4 14.5 %copy-start.34 = (f32[768]{0:T(1024)S(1)}, f32[768]{0:T(1024)}, u32[]{:S(2)}) copy-start(f32[768]{0:T(1024)} %get-tuple-element.101) | copy-start | bytes 9220
  111.9 28.3 %copy-start.36 = (f32[768]{0:T(1024)S(1)}, f32[768]{0:T(1024)}, u32[]{:S(2)}) copy-start(f32[768]{0:T(1024)} %get-tuple-element.103) | copy-start | bytes 9220
  151.9 13.6 %copy-start.7 = (f32[736,768]{1,0:T(8,128)}, f32[736,768]{1,0:T(8,128)S(1)}, u32[]{:S(2)}) copy-start(f32[736,768]{1,0:T(8,128)S(1)} %get-tuple-element.115) | copy-start | bytes 6782980
  151.9 13.6 %copy-start.24 = (f32[736]{0:T(1024)}, f32[736]{0:T(1024)S(1)}, u32[]{:S(2)}) copy-start(f32[736]{0:T(1024)S(1)} %negate_multiply_fusion.2) | copy-start | bytes 8836
  221.6 125.1 %reduce-scatter.45.cloned.1.call-start = ((), (), s32[]{:S(2)}) async-start(), calls=%async_computation.27 | async-start | bytes 442368
  222.7 151.4 %reduce-scatter.27.cloned.1.call-start = ((), (), s32[]{:S(2)}) async-start(), calls=%async_computation.14 | async-start | bytes 1474560 | tf_op jit(solution)/shard_map/reduce_scatter | solution.py:279
  226.4 190.9 %reduce-scatter.35.cloned.1.call-start = ((), (), s32[]{:S(2)}) async-start(), calls=%async_computation.22 | async-start | bytes 4423680
  226.5 22.9 %copy-start.5 = (bf16[736,768]{0,1:T(8,128)(2,1)S(1)}, bf16[736,768]{0,1:T(8,128)(2,1)}, u32[]{:S(2)}) copy-start(bf16[736,768]{0,1:T(8,128)(2,1)} %copy-done.4) | copy-start | bytes 3391492
  286.6 181.1 %reduce-scatter.33.cloned.1.call-start = ((), (), s32[]{:S(2)}) async-start(), calls=%async_computation.17 | async-start | bytes 5898240 | tf_op jit(solution)/shard_map/reduce_scatter | solution.py:279
  296.4 222.3 %reduce-scatter.29.cloned.1.call-start = ((), (), s32[]{:S(2)}) async-start(), calls=%async_computation.15 | async-start | bytes 5898240 | tf_op jit(solution)/shard_map/reduce_scatter | solution.py:279
  306.4 41.1 %copy-start.31 = (f32[3072]{0:T(1024)S(1)}, f32[3072]{0:T(1024)}, u32[]{:S(2)}) copy-start(f32[3072]{0:T(1024)} %get-tuple-element.133) | copy-start | bytes 36868
  306.5 277.5 %reduce-scatter.39.cloned.1.call-start = ((), (), s32[]{:S(2)}) async-start(), calls=%async_computation.24 | async-start | bytes 73728
  359.2 288.3 %reduce-scatter.37.cloned.1.call-start = ((), (), s32[]{:S(2)}) async-start(), calls=%async_computation.23 | async-start | bytes 442368
  376.0 308.6 %all-gather.15.cloned.1.call-start = ((), (), s32[]{:S(2)}) async-start(), calls=%async_computation.12 | async-start | bytes 5652480 | tf_op jit(solution)/shard_map/all_gather | solution.py:252
  382.9 339.4 %all-gather.13.cloned.1.call-start = ((), (), s32[]{:S(2)}) async-start(), calls=%async_computation.11 | async-start | bytes 5652480 | tf_op jit(solution)/shard_map/all_gather | solution.py:252
  383.5 406.7 %reduce-scatter.25.cloned.1.call-start = ((), (), s32[]{:S(2)}) async-start(), calls=%async_computation.13 | async-start | bytes 1327104 | tf_op jit(solution)/shard_map/reduce_scatter | solution.py:280
  421.6 97.8 %copy-start.43 = (u32[32]{0:T(128)S(1)}, u32[32]{0:T(128)}, u32[]{:S(2)}) copy-start(u32[32]{0:T(128)} %constant.151) | copy-start | bytes 388
  421.6 435.3 %reduce-scatter.41.cloned.1.call-start = ((), (), s32[]{:S(2)}) async-start(), calls=%async_computation.25 | async-start | bytes 1327104
  470.1 453.0 %reduce-scatter.31.cloned.1.call-start = ((), (), s32[]{:S(2)}) async-start(), calls=%async_computation.16 | async-start | bytes 1327104 | tf_op jit(solution)/shard_map/reduce_scatter | solution.py:280
  (35 other events, 141.7 us)
Sparse Core Ops, SparseCore 0:
  9.6 33.4 all-gather.16
  44.7 17.4 all-gather.18
  63.8 37.4 all-gather.20
  102.7 37.4 all-gather.22
  221.7 61.3 reduce-scatter.42
  286.3 60.3 reduce-scatter.44
  349.3 24.7 reduce-scatter.26
  376.8 40.4 reduce-scatter.34
  419.8 47.8 reduce-scatter.32
  470.8 47.8 reduce-scatter.28
  522.7 61.2 reduce-scatter.38
  587.1 60.4 reduce-scatter.36
  649.1 35.3 all-gather.14
  685.9 36.3 all-gather.12
  726.1 64.0 reduce-scatter.24
  793.5 63.3 reduce-scatter.40
  860.1 62.9 reduce-scatter.30
